TPU v7x, 128 devices: a whole 4x4x4 slice. The times are simulated.
128 devices in a mesh: row: 8 (over y_lo, z), col: 2 (over core), fib: 8 (over y_hi, x).
Axes of the slice: x: 4, y: 4 (y_hi: 2, y_lo: 2; y = y_hi * 2 + y_lo), z: 4, core: 2. Of those that a mesh axis runs over, the one named last changes fastest.
Arguments:
- features: bfloat16 [32768, 1024], P(('row', 'col'), 'fib'), may hold values from -6 to 6
- pre_activation: bfloat16 [32768, 1024], P(('row', 'col'), 'fib'), may hold values from -8 to 8
- out_grad: bfloat16 [32768, 1024], P(('row', 'col'), 'fib'), may hold values from -1.5 to 1.5
- weight: bfloat16 [1024, 1024], P('fib'), may hold values from -0.1875 to 0.1875
- tile_values: bfloat16 [8, 2, 128, 256, 256], P('row', 'col'), may hold values from 0.0019989014 to 0.059814453
- tile_rows: int32 [8, 2, 128], P('row', 'col'), may hold values from 0 to 15, as said below
- tile_cols: int32 [8, 2, 128], P('row', 'col'), may hold values from 0 to 63, as said below
- tile_counts: int32 [8, 2], P('row', 'col'), may hold values from 16 to 128, as said below
Outputs:
- grad_features: bfloat16 [32768, 1024], P(('row', 'col'), 'fib')
- grad_weight: float32 [1024, 1024], P('fib')
Inputs may be any that keep to these rules, and one draw needn't show every extreme that they name: `tile_rows`: within one block the used slots name distinct tiles, rows below 16. `tile_cols`: columns below 64. `tile_counts`: some block uses all 128 slots.
All inputs are finite; a program needn't handle non-finite values.
Results may differ from a plain program's by a relative error of at most 0.0058.
Values may be sent and summed in bfloat16 or wider, within the bound.
A program may use at most 128 MiB of HBM per device.

v0:
```python
import jax
import jax.numpy as jnp
from jax import lax
from jax.sharding import PartitionSpec as P


def split_up(value, dim, peers):
    before, after = (value.shape[:dim], value.shape[dim + 1 :])
    return jnp.moveaxis(value.reshape(*before, peers, -1, *after), dim, 0)


def summed_on_arrival(value, axis, dim):
    peers = lax.axis_size(axis)
    pieces = lax.all_to_all(split_up(value, dim, peers), axis, 0, 0, tiled=True)
    return jnp.sum(pieces, axis=0)


def total_of_pieces(value, axis):
    return lax.all_gather(value, axis).sum(0)


def from_everyone(value, axis):
    peers = lax.axis_size(axis)
    return lax.all_to_all(
        jnp.broadcast_to(value[None], (peers, *value.shape)), axis, 0, 0, tiled=True
    )


def joined_along(pieces, dim):
    dims = list(pieces.shape[1:])
    dims[dim] *= pieces.shape[0]
    return jnp.moveaxis(pieces, 0, dim).reshape(dims)


def gather_directly(value, axis, dim):
    pieces = from_everyone(value, axis)
    return joined_along(pieces, dim)


def place_group(running, products, target, valid, offset):
    out_tiles = running.shape[0]
    local = target - offset
    placing = (
        (local[:, None] == jnp.arange(out_tiles, dtype=jnp.int32)[None, :]) & valid[:, None]
    ).astype(jnp.float32)
    return running + jnp.einsum("st,sif->tif", placing, products, precision=lax.Precision.HIGHEST)


def group_products(tile_block, row_index, col_index, panels_all, first, slot_group, transpose):
    block_vals = lax.dynamic_slice_in_dim(tile_block, first, slot_group, 0)
    block_rows = lax.dynamic_slice_in_dim(row_index, first, slot_group, 0)
    block_cols = lax.dynamic_slice_in_dim(col_index, first, slot_group, 0)
    if transpose:
        products = jnp.einsum(
            "sij,sif->sjf", block_vals, panels_all[block_rows], preferred_element_type=jnp.float32
        )
        return (products, block_cols)
    products = jnp.einsum(
        "sij,sjf->sif", block_vals, panels_all[block_cols], preferred_element_type=jnp.float32
    )
    return (products, block_rows)


def group_total(tile_block, slot_group):
    return tile_block.shape[0] // slot_group


def tile_products(tile_block, row_index, col_index, live_count, panel_source, out_tiles, transpose):
    tile_size = tile_block.shape[1]
    feature_cols = panel_source.shape[1]
    panels_all = panel_source.reshape(-1, tile_size, feature_cols)
    slot_group = 16

    def one_block(block_index, running):
        first = block_index * slot_group
        products, target = group_products(
            tile_block, row_index, col_index, panels_all, first, slot_group, transpose
        )
        valid = first + jnp.arange(slot_group, dtype=jnp.int32) < live_count
        return place_group(running, products, target, valid, 0)

    initial = jnp.zeros((out_tiles, tile_size, feature_cols), jnp.float32)
    running = lax.fori_loop(0, group_total(tile_block, slot_group), one_block, initial)
    return running.reshape(out_tiles * tile_size, feature_cols)


def on_device(
    features, pre_activation, out_grad, weight, tile_values, tile_rows, tile_cols, tile_counts
):
    tile_block = tile_values[0, 0]
    row_index = tile_rows[0, 0]
    col_index = tile_cols[0, 0]
    live_count = tile_counts[0, 0]
    node_dev = features.shape[0]
    tile_size = tile_block.shape[1]
    row_tiles = node_dev * lax.axis_size("col") // tile_size
    col_tiles = node_dev * lax.axis_size("row") // tile_size
    column_block = lax.all_gather(features, "row", axis=0, tiled=True)
    partial_value = tile_products(
        tile_block, row_index, col_index, live_count, column_block, row_tiles, False
    )
    aggregated = summed_on_arrival(partial_value, "col", 0).astype(jnp.bfloat16)
    pre_value = pre_activation.astype(jnp.float32)
    sigmoid_value = jax.nn.sigmoid(pre_value)
    grad_local = (
        out_grad.astype(jnp.float32) * sigmoid_value * (1.0 + pre_value * (1.0 - sigmoid_value))
    ).astype(jnp.bfloat16)
    full_grad = lax.all_gather(grad_local, "fib", axis=1, tiled=True)
    weight_part = lax.dot_general(
        aggregated, full_grad, (((0,), (0,)), ((), ())), preferred_element_type=jnp.float32
    )
    grad_weight = total_of_pieces(weight_part, ("row", "col"))
    projected = lax.dot_general(
        full_grad, weight, (((1,), (1,)), ((), ())), preferred_element_type=jnp.float32
    ).astype(jnp.bfloat16)
    row_block = gather_directly(projected, "col", 0)
    transposed = tile_products(
        tile_block, row_index, col_index, live_count, row_block, col_tiles, True
    )
    grad_features = lax.psum_scatter(transposed, "row", scatter_dimension=0, tiled=True).astype(
        jnp.bfloat16
    )
    return (grad_features, grad_weight)


def solution(mesh):
    in_specs = (
        P(("row", "col"), "fib"),
        P(("row", "col"), "fib"),
        P(("row", "col"), "fib"),
        P("fib", None),
        P("row", "col", None, None, None),
        P("row", "col", None),
        P("row", "col", None),
        P("row", "col"),
    )
    out_specs = (P(("row", "col"), "fib"), P("fib", None))
    return jax.shard_map(
        on_device, mesh=mesh, in_specs=in_specs, out_specs=out_specs, check_vma=False
    )
```

profile of v0, /device:TPU:1, one launch (start us, length us, event | category | flops | bytes accessed | tf_op | source)
XLA Modules:
  0.0 379.1 jit_solution(10993640622262767804)
XLA Ops:
  8.0 2.4 fusion.26
  10.5 55.2 %all-gather.7.cloned.1.call-done = bf16[16384,128]{1,0:T(8,128)(2,1)} async-done(((bf16[2048,128]{1,0:T(8,128)(2,1)}), bf16[16384,128]{1,0:T(8,128)(2,1)}) %all-gather.7.cloned.1.call-update) | async-done | bytes 4194320 | tf_op jit(solution)/shard_map/all_gather | solution.py:98
  65.7 76.0 %while.29 = (s32[]{:T(128)}, f32[16,256,128]{2,0,1:T(8,128)S(1)}, s32[128]{0:T(128)S(1)}, s32[]{:T(128)}, bf16[128,256,256]{2,1,0:T(8,128)(2,1)}, /*index=5*/s32...) while((s32[]{:T(128)}, f32[16,256,128]{2,0,1:T(8,128)S(1)}, ...), condition=%wide.region_4.0_spmd.clone, body=%wide.region_3.0_spmd.clone.sunk | while | flops 370148960 | bytes 13636257 | solution.py:83
  66.6 2.9 gather_fusion.1
  71.8 3.4 select_add_fusion.5
  76.0 3.2 gather_fusion.1
  79.2 2.3 fusion.55
  81.5 3.4 select_add_fusion.5
  85.7 2.9 gather_fusion.1
  88.7 2.3 fusion.55
  91.0 3.4 select_add_fusion.5
  95.2 2.9 gather_fusion.1
  100.5 3.4 select_add_fusion.5
  104.7 3.0 gather_fusion.1
  110.0 3.4 select_add_fusion.5
  114.2 2.9 gather_fusion.1
  117.2 2.3 fusion.55
  119.5 3.4 select_add_fusion.5
  123.7 2.9 gather_fusion.1
  126.6 2.3 fusion.55
  128.9 3.4 select_add_fusion.5
  133.1 2.9 gather_fusion.1
  136.1 2.3 fusion.55
  138.4 3.4 select_add_fusion.5
  142.4 5.7 %all_to_all.10 = f32[2,2048,128]{2,1,0:T(8,128)S(1)} all-to-all(f32[2,2048,128]{2,1,0:T(8,128)S(1)} %bitcast.33), channel_id=1, replica_groups=mesh['row'=8,'col'=2,'fib'=8] {'col'}, dimensions={0} | all-to-all | bytes 4194304 | tf_op jit(solution)/shard_map/all_to_all | solution.py:14
  148.2 3.7 fusion.29
  152.1 3.4 convolution_convert_fusion
  155.6 4.7 %all_to_all.11 = bf16[2,2048,128]{2,1,0:T(8,128)(2,1)S(1)} all-to-all(bf16[2,2048,128]{2,1,0:T(8,128)(2,1)S(1)} %broadcast_in_dim.45), channel_id=1, replica_groups=mesh['row'=8,'col'=2,'fib'=8] {'col'}, dimensions={0} | all-to-all | bytes 2097152 | tf_op jit(solution)/shard_map/all_to_all | solution.py:24
  160.3 106.9 %while.28 = (s32[]{:T(128)}, f32[64,256,128]{2,0,1:T(8,128)}, s32[128]{0:T(128)S(1)}, s32[]{:T(128)}, bf16[128,256,256]{2,1,0:T(8,128)(2,1)}, /*index=5*/s32[128...) while((s32[]{:T(128)}, f32[64,256,128]{2,0,1:T(8,128)}, ...), condition=%wide.region_1.0_spmd.clone, body=%wide.region_0.0_spmd.clone.sunk | while | flops 675286144 | bytes 26219168 | solution.py:83
  161.9 2.4 fusion.50
  164.2 7.5 %select_add_fusion.4 = f32[64,256,128]{2,0,1:T(8,128)} fusion(f32[64,256,128]{2,0,1:T(8,128)} %get-tuple-element.426, pred[]{:T(512)S(6)} %compare.6, f32[16,256,128]{2,1,0:T(8,128)S(1)} %fusion.50, s32[16]{0:T(128)S(1)} %dynamic_slice.62, pred[16]{0:T(512)(128)(4,1)S(1)} %add_compare_fusion.4), kind=kOutput, calls=%fused_computation.2.clone.1 | convolution fusion | flops 406849536 | bytes 18874448 | tf_op jit(solution)/shard_map/while/body/eval_jaxpr/st,sif->tif/dot_general | solution.py:46
  173.3 2.4 fusion.50
  175.8 9.7 %select_add_fusion.4 = f32[64,256,128]{2,0,1:T(8,128)} fusion(f32[64,256,128]{2,0,1:T(8,128)} %get-tuple-element.426, pred[]{:T(512)S(6)} %compare.6, f32[16,256,128]{2,1,0:T(8,128)S(1)} %fusion.50, s32[16]{0:T(128)S(1)} %dynamic_slice.62, pred[16]{0:T(512)(128)(4,1)S(1)} %add_compare_fusion.4), kind=kOutput, calls=%fused_computation.2.clone.1 | convolution fusion | flops 406849536 | bytes 18874448 | tf_op jit(solution)/shard_map/while/body/eval_jaxpr/st,sif->tif/dot_general | solution.py:46
  187.1 2.4 fusion.50
  189.5 9.7 %select_add_fusion.4 = f32[64,256,128]{2,0,1:T(8,128)} fusion(f32[64,256,128]{2,0,1:T(8,128)} %get-tuple-element.426, pred[]{:T(512)S(6)} %compare.6, f32[16,256,128]{2,1,0:T(8,128)S(1)} %fusion.50, s32[16]{0:T(128)S(1)} %dynamic_slice.62, pred[16]{0:T(512)(128)(4,1)S(1)} %add_compare_fusion.4), kind=kOutput, calls=%fused_computation.2.clone.1 | convolution fusion | flops 406849536 | bytes 18874448 | tf_op jit(solution)/shard_map/while/body/eval_jaxpr/st,sif->tif/dot_general | solution.py:46
  200.8 2.4 fusion.50
  203.2 9.7 %select_add_fusion.4 = f32[64,256,128]{2,0,1:T(8,128)} fusion(f32[64,256,128]{2,0,1:T(8,128)} %get-tuple-element.426, pred[]{:T(512)S(6)} %compare.6, f32[16,256,128]{2,1,0:T(8,128)S(1)} %fusion.50, s32[16]{0:T(128)S(1)} %dynamic_slice.62, pred[16]{0:T(512)(128)(4,1)S(1)} %add_compare_fusion.4), kind=kOutput, calls=%fused_computation.2.clone.1 | convolution fusion | flops 406849536 | bytes 18874448 | tf_op jit(solution)/shard_map/while/body/eval_jaxpr/st,sif->tif/dot_general | solution.py:46
  214.4 2.4 fusion.50
  216.8 9.7 %select_add_fusion.4 = f32[64,256,128]{2,0,1:T(8,128)} fusion(f32[64,256,128]{2,0,1:T(8,128)} %get-tuple-element.426, pred[]{:T(512)S(6)} %compare.6, f32[16,256,128]{2,1,0:T(8,128)S(1)} %fusion.50, s32[16]{0:T(128)S(1)} %dynamic_slice.62, pred[16]{0:T(512)(128)(4,1)S(1)} %add_compare_fusion.4), kind=kOutput, calls=%fused_computation.2.clone.1 | convolution fusion | flops 406849536 | bytes 18874448 | tf_op jit(solution)/shard_map/while/body/eval_jaxpr/st,sif->tif/dot_general | solution.py:46
  228.0 2.4 fusion.50
  230.4 9.7 %select_add_fusion.4 = f32[64,256,128]{2,0,1:T(8,128)} fusion(f32[64,256,128]{2,0,1:T(8,128)} %get-tuple-element.426, pred[]{:T(512)S(6)} %compare.6, f32[16,256,128]{2,1,0:T(8,128)S(1)} %fusion.50, s32[16]{0:T(128)S(1)} %dynamic_slice.62, pred[16]{0:T(512)(128)(4,1)S(1)} %add_compare_fusion.4), kind=kOutput, calls=%fused_computation.2.clone.1 | convolution fusion | flops 406849536 | bytes 18874448 | tf_op jit(solution)/shard_map/while/body/eval_jaxpr/st,sif->tif/dot_general | solution.py:46
  241.6 2.4 fusion.50
  244.0 9.7 %select_add_fusion.4 = f32[64,256,128]{2,0,1:T(8,128)} fusion(f32[64,256,128]{2,0,1:T(8,128)} %get-tuple-element.426, pred[]{:T(512)S(6)} %compare.6, f32[16,256,128]{2,1,0:T(8,128)S(1)} %fusion.50, s32[16]{0:T(128)S(1)} %dynamic_slice.62, pred[16]{0:T(512)(128)(4,1)S(1)} %add_compare_fusion.4), kind=kOutput, calls=%fused_computation.2.clone.1 | convolution fusion | flops 406849536 | bytes 18874448 | tf_op jit(solution)/shard_map/while/body/eval_jaxpr/st,sif->tif/dot_general | solution.py:46
  255.2 2.4 fusion.50
  257.6 9.7 %select_add_fusion.4 = f32[64,256,128]{2,0,1:T(8,128)} fusion(f32[64,256,128]{2,0,1:T(8,128)} %get-tuple-element.426, pred[]{:T(512)S(6)} %compare.6, f32[16,256,128]{2,1,0:T(8,128)S(1)} %fusion.50, s32[16]{0:T(128)S(1)} %dynamic_slice.62, pred[16]{0:T(512)(128)(4,1)S(1)} %add_compare_fusion.4), kind=kOutput, calls=%fused_computation.2.clone.1 | convolution fusion | flops 406849536 | bytes 18874448 | tf_op jit(solution)/shard_map/while/body/eval_jaxpr/st,sif->tif/dot_general | solution.py:46
  267.2 11.5 %copy.11 = f32[64,256,128]{2,1,0:T(8,128)} copy(f32[64,256,128]{2,0,1:T(8,128)} %get-tuple-element.250) | data formatting | bytes 16777216 | tf_op jit(solution)/shard_map/while | solution.py:83
  278.8 5.1 %reduce_sum.19 = f32[128,1024]{1,0:T(8,128)} reduce(f32[16,128,1024]{2,1,0:T(8,128)} %bitcast.32, f32[]{:T(128)} %constant.71.clone.1), dimensions={0}, to_apply=%region_6.0 | reduce | flops 1966080 | bytes 8912900 | tf_op jit(solution)/shard_map/reduce_sum | solution.py:19
  283.8 86.7 %reduce-scatter.2.cloned.1.call-done = f32[2048,128]{1,0:T(8,128)} async-done(((f32[16384,128]{1,0:T(8,128)}), f32[2048,128]{1,0:T(8,128)}) %reduce-scatter.2.cloned.1.call-update) | async-done | bytes 1048592 | tf_op jit(solution)/shard_map/reduce_scatter | solution.py:120
  (99 shorter events, 29.7 us)
Async XLA Ops:
  7.2 144.9 %copy-start = (bf16[128,1024]{1,0:T(8,128)(2,1)S(1)}, bf16[128,1024]{1,0:T(8,128)(2,1)}, u32[]{:S(2)}) copy-start(bf16[128,1024]{1,0:T(8,128)(2,1)} %param.15) | copy-start | bytes 786436
  7.2 58.6 %copy-start.3 = (s32[1,1,128]{2,1,0:T(1,128)S(1)}, s32[1,1,128]{2,1,0:T(1,128)}, u32[]{:S(2)}) copy-start(s32[1,1,128]{2,1,0:T(1,128)} %param.18) | copy-start | bytes 1540
  7.2 58.6 %copy-start.2 = (s32[1,1,128]{2,1,0:T(1,128)S(1)}, s32[1,1,128]{2,1,0:T(1,128)}, u32[]{:S(2)}) copy-start(s32[1,1,128]{2,1,0:T(1,128)} %param.17) | copy-start | bytes 1540
  7.2 58.5 %all-gather.7.cloned.1.call-start = ((), (), s32[]{:S(2)}) async-start(), calls=%async_computation.5 | async-start | bytes 4718592 | tf_op jit(solution)/shard_map/all_gather | solution.py:98
  7.9 140.3 %all-gather.5.cloned.1.call-start = ((), (), s32[]{:S(2)}) async-start(), calls=%async_computation.3 | async-start | bytes 4718592 | tf_op jit(solution)/shard_map/all_gather | solution.py:108
  10.4 268.3 %all-gather.9.cloned.1.call-start = ((), (), s32[]{:S(2)}) async-start(), calls=%async_computation.6 | async-start | bytes 8912896 | tf_op jit(solution)/shard_map/all_gather | solution.py:19
  152.0 218.5 %reduce-scatter.2.cloned.1.call-start = ((), (), s32[]{:S(2)}) async-start(), calls=%async_computation.4 | async-start | bytes 9437184 | tf_op jit(solution)/shard_map/reduce_scatter | solution.py:120
  278.7 93.8 %copy-start.1 = (bf16[128,1024]{1,0:T(8,128)(2,1)S(1)}, bf16[128,1024]{1,0:T(8,128)(2,1)}, u32[]{:S(2)}) copy-start(bf16[128,1024]{1,0:T(8,128)(2,1)} %param.15) | copy-start | bytes 786436
Sparse Core Ops, SparseCore 0:
  9.7 56.0 all-gather.6
  68.5 75.8 all-gather.4
  152.1 50.9 all-gather.8
  278.8 91.6 reduce-scatter.1
where the time goes:
time: 380 us; the launch traced here: 379 us
  matrix products  147 us (39%)
  waiting for transfers between devices  143 us (38%)
  local copies, waits for them, and re-layouts  43.3 us (11%)
  other arithmetic  21.5 us (6%)
  between operations  13.9 us (4%)
  blocking collectives  10.4 us (3%)
    dot_general x16, matrix products, place_group(): jnp.einsum('st,sif->tif', placing, products, precision=lax.Precision.HIGH...  102 us
    reduce_scatter x1, waiting for transfers between devices, on_device(): lax.psum_scatter(transposed, 'row', scatter_dimension=0, tiled=True)  86.7 us
    all_gather x1, waiting for transfers between devices, on_device(): column_block = lax.all_gather(features, 'row', axis=0, tiled=True)  55.2 us
    gather x8, local copies, waits for them, and re-layouts, group_products(): panels_all[block_cols]  23.9 us
    dot_general x8, matrix products, group_products(): jnp.einsum('sij,sif->sjf', block_vals, panels_all[block_rows], preferred_...  19 us
    dot_general x8, matrix products, group_products(): jnp.einsum('sij,sjf->sif', block_vals, panels_all[block_cols], preferred_...  18.4 us
    while x2, local copies, waits for them, and re-layouts, tile_products(): lax.fori_loop(0, group_total(tile_block, slot_group), one_block, initial)  12.1 us
    lt x16, other arithmetic, one_block(): valid = first + jnp.arange(slot_group, dtype=jnp.int32) < live_count  10.4 us
  transfers between devices with their start and end apart: 4, of which 2 were waited for; matrix products, arithmetic and copies ran while one was open for 54% of the time, Pallas kernels for 0%

commit v1 on v0

--- a/solution.py
+++ b/solution.py
@@ -95,7 +95,9 @@
     tile_size = tile_block.shape[1]
     row_tiles = node_dev * lax.axis_size("col") // tile_size
     col_tiles = node_dev * lax.axis_size("row") // tile_size
-    column_block = lax.all_gather(features, "row", axis=0, tiled=True)
+    column_block = jnp.concatenate(
+        lax.all_to_all(jnp.stack(lax.axis_size("row") * [features], 0), "row", 0, 0), 0
+    )
     partial_value = tile_products(
         tile_block, row_index, col_index, live_count, column_block, row_tiles, False
     )

time: 380 us -> 396 us (1.042)
  starting transfers between devices: 0.16 us -> 7.13 us
    all_to_all x0 -> x1, waiting for transfers between devices: none -> 56.3 us  [on_device(): lax.all_to_all(jnp.stack(lax.axis_size('row') * [features], 0), 'row', 0, 0)]
    all_gather x1 -> x0, waiting for transfers between devices: 55.2 us -> none  [on_device(): column_block = lax.all_gather(features, 'row', axis=0, tiled=True)]
    all_to_all x0 -> x1, starting transfers between devices: none -> 7.01 us  [on_device(): lax.all_to_all(jnp.stack(lax.axis_size('row') * [features], 0), 'row', 0, 0)]
  transfers between devices with their start and end apart: 4 -> 4, of which waited for: 2 -> 2; matrix products, arithmetic and copies ran while one was open for 54% -> 52% of each run, Pallas kernels for 0% -> 0%
where the time goes in v1:
time: 396 us; the launch traced here: 395 us
  matrix products  147 us (37%)
  waiting for transfers between devices  145 us (37%)
  local copies, waits for them, and re-layouts  46.6 us (12%)
  other arithmetic  20.3 us (5%)
  blocking collectives  14.2 us (4%)
  between operations  13.9 us (4%)
  starting transfers between devices  7.13 us (2%)
    dot_general x16, matrix products, place_group(): jnp.einsum('st,sif->tif', placing, products, precision=lax.Precision.HIGH...  102 us
    reduce_scatter x1, waiting for transfers between devices, on_device(): lax.psum_scatter(transposed, 'row', scatter_dimension=0, tiled=True)  89 us
    all_to_all x1, waiting for transfers between devices, on_device(): lax.all_to_all(jnp.stack(lax.axis_size('row') * [features], 0), 'row', 0, 0)  56.3 us
    gather x8, local copies, waits for them, and re-layouts, group_products(): panels_all[block_cols]  23.6 us
    dot_general x8, matrix products, group_products(): jnp.einsum('sij,sif->sjf', block_vals, panels_all[block_rows], preferred_...  19.1 us
    dot_general x8, matrix products, group_products(): jnp.einsum('sij,sjf->sif', block_vals, panels_all[block_cols], preferred_...  18.3 us
    while x2, local copies, waits for them, and re-layouts, tile_products(): lax.fori_loop(0, group_total(tile_block, slot_group), one_block, initial)  12.2 us
    lt x16, other arithmetic, one_block(): valid = first + jnp.arange(slot_group, dtype=jnp.int32) < live_count  10.4 us
  transfers between devices with their start and end apart: 4, of which 2 were waited for; matrix products, arithmetic and copies ran while one was open for 52% of the time, Pallas kernels for 0%

profile of v1, /device:TPU:1, one launch (start us, length us, event | category | flops | bytes accessed | tf_op | source)
XLA Modules:
  0.0 394.8 jit_solution(16182339428216935280)
XLA Ops:
  7.2 3.6 stack.2
  10.8 7.0 %all-to-all-start.1 = ((bf16[8,2048,128]{2,1,0:T(8,128)(2,1)}), bf16[8,2048,128]{2,1,0:T(8,128)(2,1)}, u32[]{:S(2)}, u32[]{:S(2)}) async-start(bf16[8,2048,128]{2,1,0:T(8,128)(2,1)} %stack.2), calls=%async_computation.2 | async-start | bytes 8388608 | tf_op jit(solution)/shard_map/all_to_all | solution.py:99
  19.2 56.3 %all-to-all-done.1 = bf16[8,2048,128]{2,1,0:T(8,128)(2,1)} async-done(((bf16[8,2048,128]{2,1,0:T(8,128)(2,1)}), bf16[8,2048,128]{2,1,0:T(8,128)(2,1)}, u32[]{:S(2)}, u32[]{:S(2)}) %all-to-all-start.1) | async-done | bytes 4194336 | tf_op jit(solution)/shard_map/all_to_all | solution.py:99
  75.4 75.7 %while.29 = (s32[]{:T(128)}, f32[16,256,128]{2,0,1:T(8,128)S(1)}, s32[128]{0:T(128)S(1)}, s32[]{:T(128)}, bf16[128,256,256]{2,1,0:T(8,128)(2,1)}, /*index=5*/s32...) while((s32[]{:T(128)}, f32[16,256,128]{2,0,1:T(8,128)S(1)}, ...), condition=%wide.region_4.0_spmd.clone, body=%wide.region_3.0_spmd.clone.sunk | while | flops 370148960 | bytes 13636257 | solution.py:83
  76.3 2.9 gather_fusion.1
  81.5 3.4 select_add_fusion.5
  85.7 2.9 gather_fusion.1
  90.9 3.4 select_add_fusion.5
  95.2 3.0 gather_fusion.1
  100.5 3.4 select_add_fusion.5
  104.7 3.0 gather_fusion.1
  110.0 3.4 select_add_fusion.5
  114.2 2.9 gather_fusion.1
  117.1 2.3 fusion.55
  119.4 3.4 select_add_fusion.5
  123.7 2.9 gather_fusion.1
  126.6 2.3 fusion.55
  128.9 3.4 select_add_fusion.5
  133.1 2.9 gather_fusion.1
  136.0 2.3 fusion.55
  138.3 3.4 select_add_fusion.5
  142.5 2.9 gather_fusion.1
  145.5 2.3 fusion.55
  147.8 3.4 select_add_fusion.5
  151.8 9.6 %all_to_all.15 = f32[2,2048,128]{2,1,0:T(8,128)S(1)} all-to-all(f32[2,2048,128]{2,1,0:T(8,128)S(1)} %bitcast.33), channel_id=1, replica_groups=mesh['row'=8,'col'=2,'fib'=8] {'col'}, dimensions={0} | all-to-all | bytes 4194304 | tf_op jit(solution)/shard_map/all_to_all | solution.py:14
  161.6 3.7 fusion.29
  165.4 3.4 convolution_convert_fusion
  168.9 4.6 %all_to_all.16 = bf16[2,2048,128]{2,1,0:T(8,128)(2,1)S(1)} all-to-all(bf16[2,2048,128]{2,1,0:T(8,128)(2,1)S(1)} %broadcast_in_dim.45), channel_id=1, replica_groups=mesh['row'=8,'col'=2,'fib'=8] {'col'}, dimensions={0} | all-to-all | bytes 2097152 | tf_op jit(solution)/shard_map/all_to_all | solution.py:24
  173.6 107.1 %while.28 = (s32[]{:T(128)}, f32[64,256,128]{2,0,1:T(8,128)}, s32[128]{0:T(128)S(1)}, s32[]{:T(128)}, bf16[128,256,256]{2,1,0:T(8,128)(2,1)}, /*index=5*/s32[128...) while((s32[]{:T(128)}, f32[64,256,128]{2,0,1:T(8,128)}, ...), condition=%wide.region_1.0_spmd.clone, body=%wide.region_0.0_spmd.clone.sunk | while | flops 675286144 | bytes 26219168 | solution.py:83
  175.1 2.5 fusion.50
  177.7 7.5 %select_add_fusion.4 = f32[64,256,128]{2,0,1:T(8,128)} fusion(f32[64,256,128]{2,0,1:T(8,128)} %get-tuple-element.426, pred[]{:T(512)S(6)} %compare.6, f32[16,256,128]{2,1,0:T(8,128)S(1)} %fusion.50, s32[16]{0:T(128)S(1)} %dynamic_slice.62, pred[16]{0:T(512)(128)(4,1)S(1)} %add_compare_fusion.4), kind=kOutput, calls=%fused_computation.2.clone.1 | convolution fusion | flops 406849536 | bytes 18874448 | tf_op jit(solution)/shard_map/while/body/eval_jaxpr/st,sif->tif/dot_general | solution.py:46
  186.8 2.4 fusion.50
  189.1 9.7 %select_add_fusion.4 = f32[64,256,128]{2,0,1:T(8,128)} fusion(f32[64,256,128]{2,0,1:T(8,128)} %get-tuple-element.426, pred[]{:T(512)S(6)} %compare.6, f32[16,256,128]{2,1,0:T(8,128)S(1)} %fusion.50, s32[16]{0:T(128)S(1)} %dynamic_slice.62, pred[16]{0:T(512)(128)(4,1)S(1)} %add_compare_fusion.4), kind=kOutput, calls=%fused_computation.2.clone.1 | convolution fusion | flops 406849536 | bytes 18874448 | tf_op jit(solution)/shard_map/while/body/eval_jaxpr/st,sif->tif/dot_general | solution.py:46
  200.4 2.4 fusion.50
  202.8 9.7 %select_add_fusion.4 = f32[64,256,128]{2,0,1:T(8,128)} fusion(f32[64,256,128]{2,0,1:T(8,128)} %get-tuple-element.426, pred[]{:T(512)S(6)} %compare.6, f32[16,256,128]{2,1,0:T(8,128)S(1)} %fusion.50, s32[16]{0:T(128)S(1)} %dynamic_slice.62, pred[16]{0:T(512)(128)(4,1)S(1)} %add_compare_fusion.4), kind=kOutput, calls=%fused_computation.2.clone.1 | convolution fusion | flops 406849536 | bytes 18874448 | tf_op jit(solution)/shard_map/while/body/eval_jaxpr/st,sif->tif/dot_general | solution.py:46
  214.2 2.4 fusion.50
  216.6 9.7 %select_add_fusion.4 = f32[64,256,128]{2,0,1:T(8,128)} fusion(f32[64,256,128]{2,0,1:T(8,128)} %get-tuple-element.426, pred[]{:T(512)S(6)} %compare.6, f32[16,256,128]{2,1,0:T(8,128)S(1)} %fusion.50, s32[16]{0:T(128)S(1)} %dynamic_slice.62, pred[16]{0:T(512)(128)(4,1)S(1)} %add_compare_fusion.4), kind=kOutput, calls=%fused_computation.2.clone.1 | convolution fusion | flops 406849536 | bytes 18874448 | tf_op jit(solution)/shard_map/while/body/eval_jaxpr/st,sif->tif/dot_general | solution.py:46
  227.8 2.4 fusion.50
  230.2 9.7 %select_add_fusion.4 = f32[64,256,128]{2,0,1:T(8,128)} fusion(f32[64,256,128]{2,0,1:T(8,128)} %get-tuple-element.426, pred[]{:T(512)S(6)} %compare.6, f32[16,256,128]{2,1,0:T(8,128)S(1)} %fusion.50, s32[16]{0:T(128)S(1)} %dynamic_slice.62, pred[16]{0:T(512)(128)(4,1)S(1)} %add_compare_fusion.4), kind=kOutput, calls=%fused_computation.2.clone.1 | convolution fusion | flops 406849536 | bytes 18874448 | tf_op jit(solution)/shard_map/while/body/eval_jaxpr/st,sif->tif/dot_general | solution.py:46
  241.4 2.4 fusion.50
  243.8 9.7 %select_add_fusion.4 = f32[64,256,128]{2,0,1:T(8,128)} fusion(f32[64,256,128]{2,0,1:T(8,128)} %get-tuple-element.426, pred[]{:T(512)S(6)} %compare.6, f32[16,256,128]{2,1,0:T(8,128)S(1)} %fusion.50, s32[16]{0:T(128)S(1)} %dynamic_slice.62, pred[16]{0:T(512)(128)(4,1)S(1)} %add_compare_fusion.4), kind=kOutput, calls=%fused_computation.2.clone.1 | convolution fusion | flops 406849536 | bytes 18874448 | tf_op jit(solution)/shard_map/while/body/eval_jaxpr/st,sif->tif/dot_general | solution.py:46
  255.0 2.4 fusion.50
  257.4 9.7 %select_add_fusion.4 = f32[64,256,128]{2,0,1:T(8,128)} fusion(f32[64,256,128]{2,0,1:T(8,128)} %get-tuple-element.426, pred[]{:T(512)S(6)} %compare.6, f32[16,256,128]{2,1,0:T(8,128)S(1)} %fusion.50, s32[16]{0:T(128)S(1)} %dynamic_slice.62, pred[16]{0:T(512)(128)(4,1)S(1)} %add_compare_fusion.4), kind=kOutput, calls=%fused_computation.2.clone.1 | convolution fusion | flops 406849536 | bytes 18874448 | tf_op jit(solution)/shard_map/while/body/eval_jaxpr/st,sif->tif/dot_general | solution.py:46
  268.6 2.4 fusion.50
  271.0 9.7 %select_add_fusion.4 = f32[64,256,128]{2,0,1:T(8,128)} fusion(f32[64,256,128]{2,0,1:T(8,128)} %get-tuple-element.426, pred[]{:T(512)S(6)} %compare.6, f32[16,256,128]{2,1,0:T(8,128)S(1)} %fusion.50, s32[16]{0:T(128)S(1)} %dynamic_slice.62, pred[16]{0:T(512)(128)(4,1)S(1)} %add_compare_fusion.4), kind=kOutput, calls=%fused_computation.2.clone.1 | convolution fusion | flops 406849536 | bytes 18874448 | tf_op jit(solution)/shard_map/while/body/eval_jaxpr/st,sif->tif/dot_general | solution.py:46
  280.6 11.5 %copy.11 = f32[64,256,128]{2,1,0:T(8,128)} copy(f32[64,256,128]{2,0,1:T(8,128)} %get-tuple-element.250) | data formatting | bytes 16777216 | tf_op jit(solution)/shard_map/while | solution.py:83
  292.2 5.1 %reduce_sum.19 = f32[128,1024]{1,0:T(8,128)} reduce(f32[16,128,1024]{2,1,0:T(8,128)} %bitcast.32, f32[]{:T(128)} %constant.71.clone.1), dimensions={0}, to_apply=%region_6.0 | reduce | flops 1966080 | bytes 8912900 | tf_op jit(solution)/shard_map/reduce_sum | solution.py:19
  297.2 89.0 %reduce-scatter.2.cloned.1.call-done = f32[2048,128]{1,0:T(8,128)} async-done(((f32[16384,128]{1,0:T(8,128)}), f32[2048,128]{1,0:T(8,128)}) %reduce-scatter.2.cloned.1.call-update) | async-done | bytes 1048592 | tf_op jit(solution)/shard_map/reduce_scatter | solution.py:122
  (103 shorter events, 32.5 us)
Async XLA Ops:
  7.2 158.2 %copy-start = (bf16[128,1024]{1,0:T(8,128)(2,1)S(1)}, bf16[128,1024]{1,0:T(8,128)(2,1)}, u32[]{:S(2)}) copy-start(bf16[128,1024]{1,0:T(8,128)(2,1)} %param.15) | copy-start | bytes 786436
  10.8 7.1 %copy-start.2 = (bf16[2048,128]{1,0:T(8,128)(2,1)S(1)}, bf16[2048,128]{1,0:T(8,128)(2,1)}, u32[]{:S(2)}) copy-start(bf16[2048,128]{1,0:T(8,128)(2,1)} %param.13) | copy-start | bytes 1572868
  10.8 7.1 %copy-start.3 = (bf16[2048,128]{1,0:T(8,128)(2,1)S(1)}, bf16[2048,128]{1,0:T(8,128)(2,1)}, u32[]{:S(2)}) copy-start(bf16[2048,128]{1,0:T(8,128)(2,1)} %param.14) | copy-start | bytes 1572868
  10.8 64.7 %all-to-all-start.1 = ((bf16[8,2048,128]{2,1,0:T(8,128)(2,1)}), bf16[8,2048,128]{2,1,0:T(8,128)(2,1)}, u32[]{:S(2)}, u32[]{:S(2)}) async-start(bf16[8,2048,128]{2,1,0:T(8,128)(2,1)} %stack.2), calls=%async_computation.2 | async-start | bytes 8388608 | tf_op jit(solution)/shard_map/all_to_all | solution.py:99
  17.8 57.7 %copy-start.4 = (s32[1,1,128]{2,1,0:T(1,128)S(1)}, s32[1,1,128]{2,1,0:T(1,128)}, u32[]{:S(2)}) copy-start(s32[1,1,128]{2,1,0:T(1,128)} %param.17) | copy-start | bytes 1540
  17.8 57.6 %copy-start.5 = (s32[1,1,128]{2,1,0:T(1,128)S(1)}, s32[1,1,128]{2,1,0:T(1,128)}, u32[]{:S(2)}) copy-start(s32[1,1,128]{2,1,0:T(1,128)} %param.18) | copy-start | bytes 1540
  17.8 143.8 %all-gather.4.cloned.1.call-start = ((), (), s32[]{:S(2)}) async-start(), calls=%async_computation.4 | async-start | bytes 4718592 | tf_op jit(solution)/shard_map/all_gather | solution.py:110
  19.1 273.0 %all-gather.6.cloned.1.call-start = ((), (), s32[]{:S(2)}) async-start(), calls=%async_computation.6 | async-start | bytes 8912896 | tf_op jit(solution)/shard_map/all_gather | solution.py:19
  165.3 220.9 %reduce-scatter.2.cloned.1.call-start = ((), (), s32[]{:S(2)}) async-start(), calls=%async_computation.5 | async-start | bytes 9437184 | tf_op jit(solution)/shard_map/reduce_scatter | solution.py:122
  292.2 96.1 %copy-start.1 = (bf16[128,1024]{1,0:T(8,128)(2,1)S(1)}, bf16[128,1024]{1,0:T(8,128)(2,1)}, u32[]{:S(2)}) copy-start(bf16[128,1024]{1,0:T(8,128)(2,1)} %param.15) | copy-start | bytes 786436
Sparse Core Ops, SparseCore 0:
  21.4 90.0 all-gather.3
  165.5 53.3 all-gather.5
  292.2 93.9 reduce-scatter.1
